TPU v7x, 32 devices: a whole 2x2x4 slice. The times are simulated.
32 devices in a mesh: seq: 8 (over z, y), state: 4 (over x, core).
Axes of the slice: x: 2, y: 2, z: 4, core: 2. Of those that a mesh axis runs over, the one named last changes fastest.
Arguments:
- layer_input: bfloat16 [2048, 1024], P('seq'), may hold values from -6 to 6
- out_grad: bfloat16 [2048, 1024], P('seq'), may hold values from -6 to 6
- doc_starts: int32 [8], replicated, may hold values from 0 to 2047, as said below
- real_mask: int32 [2048], replicated, may hold values from 0 to 1, as said below
- norm_gain: float32 [1024], replicated, may hold values from 0.5 to 1.5
- attention_input_rows: bfloat16 [1024, 768], replicated, may hold values from -0.25 to 0.25
- mixer_in: bfloat16 [1024, 2, 1536], replicated, may hold values from -0.1875 to 0.1875
- state_in: bfloat16 [1024, 2, 128], P(None, None, 'state'), may hold values from -0.046875 to 0.046875
- step_in: bfloat16 [1024, 24], replicated, may hold values from -0.1875 to 0.1875
- conv_mixer: float32 [4, 1536], replicated, may hold values from -3 to 3
- conv_state: float32 [4, 2, 128], P(None, None, 'state'), may hold values from -3 to 3
- step_bias: float32 [24], replicated, may hold values from -1.5 to 0.5
- decay_rate: float32 [24], replicated, may hold values from 0 to 1, as said below
- skip_gain: float32 [24], replicated, may hold values from 0.5 to 1.5
- gated_gain: float32 [1536], replicated, may hold values from 0.5 to 1.5
- joint_out: bfloat16 [2048, 1024], replicated, may hold values from -0.15625 to 0.15625
- mlp_gain: float32 [1024], replicated, may hold values from 0.5 to 1.5
- gate_up: bfloat16 [1024, 2, 2048], P(None, None, 'state'), may hold values from -0.1875 to 0.1875
- down_weight: bfloat16 [1024, 2048], P(None, 'state'), may hold values from -0.125 to 0.125
Outputs:
- layer_output: bfloat16 [2048, 1024], P('seq')
- input_grad: float32 [2048, 1024], P('seq')
- grad_norm_gain: float32 [1024], P('seq')
- grad_attention_in: float32 [1024, 768], P('seq')
- grad_mixer_in: float32 [1024, 2, 1536], P('seq')
- grad_state_in: float32 [1024, 2, 128], P('seq', None, 'state')
- grad_step_in: float32 [1024, 24], P('seq')
- grad_conv_mixer: float32 [4, 1536], replicated
- grad_conv_state: float32 [4, 2, 128], P(None, None, 'state')
- grad_step_bias: float32 [24], replicated
- grad_decay_rate: float32 [24], replicated
- grad_skip_gain: float32 [24], replicated
- grad_gated_gain: float32 [1536], P('seq')
- grad_joint_out: float32 [2048, 1024], P('seq')
- grad_mlp_gain: float32 [1024], P('seq')
- grad_gate_up: float32 [1024, 2, 2048], P('seq', None, 'state')
- grad_down_weight: float32 [1024, 2048], P('seq', 'state')
Inputs may be any that keep to these rules, and one draw needn't show every extreme that they name: doc_starts[0] is 0 and the entries rise strictly; document k covers doc_starts[k] up to the next entry, the last one up to 2048; entry 1 is at most 128 and entry 2 is at least 1792. `real_mask`: pad is the last 1 to 64 positions of the row, and in each document a tail of at most a quarter of its length; all other positions are real. `decay_rate`: positive rates.
All inputs are finite; a program needn't handle non-finite values.
Results may differ from a plain program's by a relative error of at most 0.015.
Values may be sent and summed in bfloat16 or wider, within the bound.
A program may use at most 320 MiB of HBM per device.

v0:
```python
import functools
import math
import types

import jax
import jax.numpy as jnp
from jax import lax
from jax.experimental import pallas as pl
from jax.experimental.pallas import tpu as pltpu
from jax.sharding import PartitionSpec as P

QUERY_HEADS = 8
KEY_VALUE_HEADS = 2
HEAD_SIZE = 64
NH = 24
HDM = 64
KC = 4
EPSILON = 1e-05
ROPE_BASE = 10000.0
FINE, LEFT, RIGHT = 1, 2, 3
F32 = jnp.float32
BF16 = jnp.bfloat16
LANES = 128
HALO = 16
FAR = -1e30
MESH = pl.DeviceIdType.MESH
SEQ, STATE = "seq", "state"
VMEM_LIMIT = 63 << 20


def parts(v):
    high = v.astype(BF16)
    return high, (v - high.astype(F32)).astype(BF16)


def product(dims, a, b, mode):
    dot = lambda u, v: lax.dot_general(u, v, (dims, ((), ())), preferred_element_type=F32)
    if mode is None:
        return dot(a, b)
    if mode == LEFT:
        high, low = parts(b)
        a = a.astype(BF16)
        return dot(a, high) + dot(a, low)
    if mode == RIGHT:
        high, low = parts(a)
        b = b.astype(BF16)
        return dot(high, b) + dot(low, b)
    a_high, a_low = parts(a)
    b_high, b_low = parts(b)
    return dot(a_high, b_high) + (dot(a_high, b_low) + dot(a_low, b_high))


def nn(a, b, mode=None):
    return product(((1,), (0,)), a, b, mode)


def nt(a, b, mode=None):
    return product(((1,), (1,)), a, b, mode)


def tn(a, b, mode=None):
    return product(((0,), (0,)), a, b, mode)


def sigmoid(v):
    return 1.0 / (1.0 + jnp.exp(-v))


def silu(v):
    return v * sigmoid(v)


def silu_slope(v):
    s = sigmoid(v)
    return s * (1.0 + v * (1.0 - s))


def softplus(v):
    return jnp.maximum(v, 0.0) + jnp.log1p(jnp.exp(-jnp.abs(v)))


def iota(shape, dim):
    return lax.broadcasted_iota(jnp.int32, shape, dim)


def doc_of(starts, pos):
    found = jnp.full(pos.shape, -1, jnp.int32)
    for start in starts:
        found = found + (pos >= start).astype(jnp.int32)
    return found


def roll(v, shift):
    return pltpu.roll(v, shift, 1)


def rope(v, cosine, sine, direction):
    first = (iota(v.shape, 1) % HEAD_SIZE) < HEAD_SIZE // 2
    half = HEAD_SIZE // 2
    partner = jnp.where(first, -roll(v, v.shape[1] - half), roll(v, half))
    return v * cosine + partner * (direction * sine)


def expander(width):
    return (iota((LANES, width), 1) // HDM == iota((LANES, width), 0)).astype(F32)


def masks_of(starts, first_row, rows):
    pos = first_row + iota((rows, 1), 0)
    doc = doc_of(starts, pos)
    masks = [(doc_of(starts, pos - (KC - 1 - k)) == doc).astype(F32) for k in range(KC)]
    return doc, masks


def push(src, dst, send_sem, recv_sem, device):
    copy = pltpu.make_async_remote_copy(
        src_ref=src,
        dst_ref=dst,
        send_sem=send_sem,
        recv_sem=recv_sem,
        device_id=device,
        device_id_type=MESH,
    )
    copy.start()
    return copy


def greet(n, ns, s, t):
    barrier = pltpu.get_barrier_semaphore()

    def seq_turn(k, carried):
        pl.semaphore_signal(barrier, inc=1, device_id={SEQ: lax.rem(s + k, n)}, device_id_type=MESH)
        return carried

    lax.fori_loop(1, n, seq_turn, 0)
    for k in range(1, ns):
        other = lax.rem(t + k, ns)
        pl.semaphore_signal(barrier, inc=1, device_id={STATE: other}, device_id_type=MESH)
        pl.semaphore_signal(
            barrier, inc=1, device_id={SEQ: lax.rem(s + 1, n), STATE: other}, device_id_type=MESH
        )
    return lambda: pl.semaphore_wait(barrier, n - 1 + 2 * (ns - 1))


def conv_ref(ext_ref, taps, masks, rows):
    total = 0.0
    for k in range(KC):
        at = HALO - KC + 1 + k
        total = total + ext_ref[at : at + rows, :] * taps[k : k + 1] * masks[k]
    return total


class Carry:
    def __init__(self, refs, window, n, s, direction, rows_e):
        self.n, self.s, self.direction, self.rows_e = n, s, direction, rows_e
        self.tx, self.rx, self.thr_tx, self.thr_rx = refs.tx, refs.rx, refs.thr_tx, refs.thr_rx
        self.send, self.recv = refs.sem
        self.thr_send, self.thr_recv = refs.thr_sem
        self.total, self.thr = window
        self.count = carry_steps(n)

    def place(self, slot):
        return (1, 0) if slot == 0 else (2, 0) if slot == 1 else (1 << (slot - 1), slot - 1)

    def copies(self, slot, d, source):
        to = lax.rem(self.s + self.direction * d + self.n, self.n)
        make = lambda src, dst, a, b: pltpu.make_async_remote_copy(
            src_ref=src,
            dst_ref=dst,
            send_sem=a,
            recv_sem=b,
            device_id={SEQ: to},
            device_id_type=MESH,
        )
        return (
            make(self.tx.at[source], self.rx.at[slot], self.send.at[slot], self.recv.at[slot]),
            make(
                self.thr_tx.at[source],
                self.thr_rx.at[slot],
                self.thr_send.at[slot],
                self.thr_recv.at[slot],
            ),
        )

    def inside(self, index):
        return (index >= 0) & (index < self.n)

    def start(self, slot, d, source):
        @pl.when(self.inside(self.s + self.direction * d))
        def _():
            for copy in self.copies(slot, d, source):
                copy.start()

    def finish(self):
        for slot in range(self.count):
            d, source = self.place(slot)

            @pl.when(self.inside(self.s + self.direction * d))
            def _():
                for copy in self.copies(slot, d, source):
                    copy.wait_send()

    def begin(self, part, thr):
        self.tx[0] = part.astype(BF16)
        self.thr_tx[0] = thr
        self.total[...] = jnp.zeros(self.total.shape, F32)
        self.thr[...] = jnp.ones(self.thr.shape, F32)
        for slot in range(min(2, self.count)):
            self.start(slot, *self.place(slot))

    def join(self, slot, d, source):
        @pl.when(self.inside(self.s - self.direction * d))
        def _():
            for copy in self.copies(slot, d, source):
                copy.wait_recv()
            column = nt(self.rows_e, self.thr[...], LEFT)[:, :1]
            self.total[...] += column * self.rx[slot].astype(F32)
            self.thr[...] = self.thr[...] * self.thr_rx[slot]

        @pl.when(jnp.logical_not(self.inside(self.s - self.direction * d)))
        def _():
            self.thr[...] = jnp.zeros(self.thr.shape, F32)

    def pass_on(self, slot, d):
        self.tx[slot - 1] = self.total[...].astype(BF16)
        self.thr_tx[slot - 1] = self.thr[...]
        self.start(slot, d, slot - 1)

    def advance(self, slot):
        self.join(slot, *self.place(slot))
        if 1 <= slot < self.count - 1:
            self.pass_on(slot + 1, 1 << slot)

    def rest(self, first):
        if first >= self.count:
            return
        for slot in range(first, min(2, self.count)):
            self.advance(slot)
        first = max(first, 2)

        def turn(slot, d):
            self.join(slot, d, slot - 1)
            self.pass_on(slot + 1, 2 * d)
            return 2 * d

        if first < self.count:
            lax.fori_loop(first, self.count - 1, turn, 1 << (first - 1))
            self.join(self.count - 1, 1 << (self.count - 2), self.count - 2)


def carry_steps(n):
    return 1 if n <= 2 else 1 + (n - 2).bit_length()


def expand_rows(width):
    return (iota((width, LANES), 0) // HDM == iota((width, LANES), 1)).astype(F32)


def link_of(linked, cum, cum_t, h):
    return jnp.exp(jnp.where(linked, cum[:, h : h + 1] - cum_t[h : h + 1, :], FAR))


def send_to(sems, k, src, dst, device):
    send, recv = sems
    return push(src, dst, send.at[k], recv.at[k], device)


def row_sums(values):
    return nt(jnp.ones((8, values.shape[1]), F32), values, LEFT)


def as_column(row):
    first = (iota((8, LANES), 0) == 0).astype(F32)
    return tn(row, first, RIGHT)[:, :1]


def share_rows(refs, ns, t, row):
    tx, rx = refs.tx, refs.rx
    tx[...] = row
    copies = [
        send_to(refs.sem, k - 1, tx, rx.at[k - 1], {STATE: lax.rem(t + k, ns)})
        for k in range(1, ns)
    ]

    def wait():
        total = tx[...]
        for k in range(1, ns):
            copies[k - 1].wait_recv()
            total = total + rx[k - 1]
        return total

    return copies, wait


class RowScatter:
    def __init__(self, refs, sem, t):
        self.sem, self.t = sem, t
        self.tx, self.rx, self.mid = refs.tx, refs.rx, refs.mid
        self.odd, self.far = lax.rem(t, 2), t // 2
        self.copies = []

    def start(self, part):
        rows = self.tx.shape[1]
        part = part.astype(BF16)
        for k in range(4):
            self.tx[(k % 2) * 2 + k // 2] = part[rows * k : rows * (k + 1)]
        theirs = self.tx.at[pl.ds(2 - 2 * self.odd, 2)]
        self.copies.append(
            send_to(self.sem, 0, theirs, self.rx.at[pl.ds(0, 2)], {STATE: sibling(self.t)})
        )

    def middle(self):
        self.copies[0].wait_recv()
        away = 1 - self.far
        self.mid[...] = (
            self.tx[2 * self.odd + away].astype(F32) + self.rx[away].astype(F32)
        ).astype(BF16)
        self.copies.append(
            send_to(self.sem, 1, self.mid, self.rx.at[2], {STATE: lax.rem(self.t + 2, 4)})
        )

    def finish(self):
        total = self.tx[2 * self.odd + self.far].astype(F32) + self.rx[self.far].astype(F32)
        self.copies[1].wait_recv()
        return total + self.rx[2].astype(F32)


class Gather:
    def __init__(self, block, sem, t):
        self.block, self.sem, self.t = block, sem, t
        own = block(t)
        self.copies = [
            send_to(sem, 0, own, own, {STATE: sibling(t)}),
            send_to(sem, 1, own, own, {STATE: lax.rem(t + 2, 4)}),
        ]

    def middle(self):
        self.copies[1].wait_recv()
        block = self.block(lax.rem(self.t + 2, 4))
        self.copies.append(send_to(self.sem, 2, block, block, {STATE: sibling(self.t)}))

    def finish(self):
        self.copies[0].wait_recv()
        self.copies[2].wait_recv()


def gather(every, sem, t, own):
    every[t] = own
    return Gather(lambda index: every.at[index], sem, t)


def sibling(t):
    return t + 1 - 2 * lax.rem(t, 2)


def levels_of(n):
    return n.bit_length() - 1


def bits_of(n, swapped):
    order = list(range(levels_of(n)))
    if swapped and len(order) > 1:
        order[0], order[1] = order[1], order[0]
    return order


class HalvingSum:
    def __init__(self, refs, n, s, swapped=False):
        self.sem, self.n, self.s = refs.sem, n, s
        self.bits = bits_of(n, swapped)
        self.src, self.rx = refs.src, refs.rx
        self.copies = []

    def owner(self, p):
        top = len(self.bits) - 1
        return sum(((p >> (top - level)) & 1) << bit for level, bit in enumerate(self.bits))

    def block_of(self, index):
        top = len(self.bits) - 1
        return sum(((index >> bit) & 1) << (top - level) for level, bit in enumerate(self.bits))

    def fill(self, column, values):
        rows = self.src.shape[1]
        width = values.shape[1]
        for p in range(self.n):
            at = rows * self.owner(p)
            self.src[p, :, column : column + width] = values[at : at + rows]

    def parts(self, level):
        half = self.n >> (level + 1)
        mine = lax.rem(self.s // (1 << self.bits[level]), 2)
        if level == 0:
            return self.src, 0, half, mine
        return self.rx, self.n - (self.n >> (level - 1)), half, mine

    def start(self, level=0):
        buffer, base, half, mine = self.parts(level)
        to = self.s + (1 - 2 * mine) * (1 << self.bits[level])
        here = self.n - (self.n >> level)
        self.copies.append(
            send_to(
                self.sem,
                level,
                buffer.at[pl.ds(base + (1 - mine) * half, half)],
                self.rx.at[pl.ds(here, half)],
                {SEQ: to},
            )
        )

    def step(self, level):
        buffer, base, half, mine = self.parts(level)
        self.copies[level].wait_recv()
        here = self.n - (self.n >> level)

        def turn(i, carried):
            kept = buffer[base + mine * half + i].astype(F32)
            self.rx[here + i] = (kept + self.rx[here + i].astype(F32)).astype(BF16)
            return carried

        lax.fori_loop(0, half, turn, 0)
        if level + 1 < len(self.bits):
            self.start(level + 1)

    def result(self):
        return self.rx[self.n - 2]


def named(value):
    if isinstance(value, dict):
        return types.SimpleNamespace(**{key: named(item) for key, item in value.items()})
    return value


def layer_kernel(n, ns, trees, *flat):
    refs, at = types.SimpleNamespace(), 0
    for tree in trees:
        part = jax.tree.unflatten(tree, flat[at : at + tree.num_leaves])
        at += tree.num_leaves
        refs.__dict__.update(named(part).__dict__)
    x, normed, inv1 = refs.x, refs.normed, refs.inv1
    w_mix, w_qkv, w_joint, w_gu, down = refs.w_mix, refs.w_qkv, refs.w_joint, refs.w_gu, refs.down
    grad = refs.grad
    w_step = refs.w_step
    T, D = x.shape
    t, s = lax.axis_index(STATE), lax.axis_index(SEQ)
    joined = refs.jall_all.at[t]
    C = w_mix.shape[2]
    QC = 2 * HEAD_SIZE
    AQ = QUERY_HEADS * HEAD_SIZE
    NW = refs.st_own.shape[1]
    HL = NH // ns
    N = NW * ns
    TO = T // ns
    DM = C * ns
    F = down.shape[1]
    pairs = C // LANES
    scale = 1.0 / math.sqrt(HEAD_SIZE)
    state_peer = lambda k: {STATE: lax.rem(t + k, ns)}
    own_c = pl.ds(pl.multiple_of(C * t, LANES), C)
    loads = [
        pltpu.make_async_copy(src, dst, refs.load[k])
        for k, (src, dst) in enumerate(
            [
                (refs.w_att.at[:, pl.ds(pl.multiple_of(QC * t, LANES), QC)], w_qkv.at[:, pl.ds(0, QC)]),
                (refs.w_att.at[:, pl.ds(AQ, 2 * QC)], w_qkv.at[:, pl.ds(QC, 2 * QC)]),
                (refs.w_mix_in.at[:, :, own_c], refs.raw),
                (refs.joint.at[pl.ds(pl.multiple_of(QC * t, QC), QC)], w_joint.at[pl.ds(0, QC)]),
                (refs.joint.at[pl.ds(pl.multiple_of(AQ + C * t, LANES), C)], w_joint.at[pl.ds(QC, C)]),
                (refs.g, grad),
                (refs.down_in, down),
                (refs.w_gu_in.at[:, :, pl.ds(0, F // 2)], refs.raw.at[:, :, pl.ds(0, F // 2)]),
                (refs.w_gu_in.at[:, :, pl.ds(F // 2, F // 2)], refs.raw.at[:, :, pl.ds(0, F // 2)]),
            ]
        )
    ]
    for load in loads[:-2]:
        load.start()
    lanes_row = iota((1, LANES), 1)
    blank = jnp.zeros((1, LANES), F32)
    met = greet(n, ns, s, t)
    bias_row, rate_row = blank, blank
    skip_row = jnp.zeros((1, C), F32)
    heads_row = iota((1, C), 1) // HDM
    for h in range(HL):
        bias_row = jnp.where(lanes_row == h, refs.step_bias[HL * t + h], bias_row)
        rate_row = jnp.where(lanes_row == h, refs.decay_rate[HL * t + h], rate_row)
        skip_row = jnp.where(heads_row == h, refs.skip_gain[HL * t + h], skip_row)
    taps_mix = refs.conv_mixer[:, own_c]
    ggain_row = jnp.concatenate(
        [refs.ggain[pl.ds(C // LANES * t + k, 1), :] for k in range(C // LANES)], axis=1
    )
    pick = (iota((NH, LANES), 0) == HL * t + iota((NH, LANES), 1)) & (iota((NH, LANES), 1) < HL)
    pick = pick.astype(F32)
    refs.taps8[...] = jnp.zeros(refs.taps8.shape, F32)
    for c in range(2):
        refs.taps8[:KC, NW * c : NW * (c + 1)] = refs.conv_state[:, c, :]
    eye8 = (iota((8, LANES), 0) == iota((8, LANES), 1)).astype(F32)
    taps_cols = tn(refs.taps8[...], eye8, RIGHT)
    for c in range(2):
        refs.taps_st[c] = taps_cols[NW * c : NW * (c + 1)]
    sent = []
    mine = pl.ds(pl.multiple_of(NW * t, NW), NW)
    refs.st_all[:, mine, :] = refs.st_own[...]
    refs.taps_all[:, mine, :] = refs.taps_st[...]

    first_row = s * T
    starts = [refs.doc_starts[k] for k in range(refs.doc_starts.shape[0])]
    doc, masks = masks_of(starts, first_row, T)
    tiles = T // LANES

    def code_turn(j, carried):
        for i in range(tiles):
            real = refs.real[pl.ds(tiles * j + i, 1), :]
            ids = doc_of(starts, j * T + i * LANES + iota((1, LANES), 1))
            refs.codes[pl.ds(tiles * j + i, 1), :] = jnp.where(real > 0, ids, -7)
        return carried

    lax.fori_loop(0, n, code_turn, 0)

    def code_of(j):
        return jnp.concatenate([refs.codes[pl.ds(tiles * j + i, 1), :] for i in range(tiles)], axis=1)

    real_col = as_column(jnp.broadcast_to((code_of(s) >= 0).astype(F32), (8, T)))
    firsts = jnp.zeros((T, 1), jnp.int32)
    places = first_row + iota((T, 1), 0)
    for start in starts:
        firsts = jnp.where(places >= start, start, firsts)
    powers = (iota((1, LANES), 1) % (HEAD_SIZE // 2)).astype(F32) * (2.0 / HEAD_SIZE)
    angles = (places - firsts).astype(F32) * jnp.exp(-math.log(ROPE_BASE) * powers)
    cosine, sine = jnp.cos(angles), jnp.sin(angles)
    doc_row = doc_of(starts, first_row + iota((1, T), 1))
    lane = iota((T, LANES), 1)
    low = lane < HEAD_SIZE
    ngain = refs.ngain[...]

    met()
    halo_copy = pltpu.make_async_remote_copy(
        src_ref=x.at[pl.ds(T - HALO, HALO)],
        dst_ref=refs.halo_rx,
        send_sem=refs.halo[0].at[0],
        recv_sem=refs.halo[1].at[0],
        device_id={SEQ: lax.rem(s + 1, n)},
        device_id_type=MESH,
    )

    @pl.when(s + 1 < n)
    def _():
        halo_copy.start()

    columns = lambda every: lambda i: every.at[:, pl.ds(pl.multiple_of(NW * i, NW), NW), :]
    st_gather = Gather(columns(refs.st_all), refs.st, t)
    taps_gather = Gather(columns(refs.taps_all), refs.taps, t)
    xf = x[...].astype(F32)
    inv = lax.rsqrt(jnp.mean(xf * xf, axis=1, keepdims=True) + EPSILON)
    inv1[...] = inv
    normed[HALO:, :] = (xf * inv * ngain).astype(BF16)
    main = normed[HALO:, :]
    loads[0].wait()
    loads[1].wait()
    qkv = nn(main, w_qkv[...])
    q = (rope(qkv[:, :QC], cosine, sine, 1.0).astype(BF16) * scale).astype(F32)
    kcos, ksin = jnp.where(low, cosine, 1.0), jnp.where(low, sine, 0.0)
    kv_all = refs.kv_all
    group = t // 2
    both_k, both_v = qkv[:, QC : 2 * QC], qkv[:, 2 * QC :]
    own_kv = jnp.where(
        low,
        jnp.where(group == 0, both_k, roll(both_k, HEAD_SIZE)),
        jnp.where(group == 0, roll(both_v, HEAD_SIZE), both_v),
    )
    kv_all[s] = rope(own_kv, kcos, ksin, 1.0).astype(BF16)

    core = lax.rem(t, 2)
    H2 = T // 2
    own_half = pl.ds(pl.multiple_of(H2 * core, H2), H2)
    other_half = pl.ds(pl.multiple_of(H2 * (1 - core), H2), H2)

    def kv_copy(k):
        return pltpu.make_async_remote_copy(
            src_ref=kv_all.at[s, own_half],
            dst_ref=kv_all.at[s, own_half],
            send_sem=refs.kv[0].at[k - 1],
            recv_sem=refs.kv[1].at[k - 1],
            device_id={SEQ: lax.rem(s + k, n)},
            device_id_type=MESH,
        )

    def kv_pair(k):
        block = kv_all.at[s - k, own_half]
        return pltpu.make_async_remote_copy(
            src_ref=block,
            dst_ref=block,
            send_sem=refs.kv_fwd[0].at[k - 1],
            recv_sem=refs.kv_fwd[1].at[k - 1],
            device_id={STATE: sibling(t)},
            device_id_type=MESH,
        )

    def kv_turn(k, carried):
        kv_copy(k).start()
        return carried

    lax.fori_loop(1, n - s, kv_turn, 0)
    refs.q2[:T, :] = jnp.where(low, q, 0.0).astype(BF16)
    refs.q2[T:, :] = jnp.where(low, roll(q, HEAD_SIZE), 0.0).astype(BF16)
    raw = nn(nt(main, w_step[...]), pick, RIGHT) + bias_row

    doc2 = jnp.concatenate([doc, doc], axis=0)
    m_ref, l_ref, acc_ref = refs.m_acc, refs.l_acc, refs.o_acc
    m_ref[...] = jnp.full(m_ref.shape, FAR, F32)
    l_ref[...] = jnp.zeros(l_ref.shape, F32)
    acc_ref[...] = jnp.zeros(acc_ref.shape, F32)

    def allowed_at(j, diagonal):
        allowed = code_of(j) == doc2
        if diagonal:
            rows2 = jnp.concatenate([iota((T, T), 0)] * 2, axis=0)
            cols2 = iota((2 * T, T), 1)
            allowed = (allowed & (cols2 <= rows2)) | (cols2 == rows2)
        return allowed

    def attend(j, diagonal):
        block = kv_all[j]
        scores = jnp.where(allowed_at(j, diagonal), nt(refs.q2[...], block), FAR)
        m = m_ref[...]
        m_new = jnp.maximum(m, jnp.max(scores, axis=1, keepdims=True))
        shrink = jnp.exp(m - m_new)
        p = jnp.exp(scores - m_new)
        l_ref[...] = l_ref[...] * shrink + jnp.sum(p, axis=1, keepdims=True)
        acc_ref[...] = acc_ref[...] * shrink + nn(p.astype(BF16), block)
        m_ref[...] = m_new

    def attend_turn(k, carried):
        @pl.when(k < s)
        def _():
            kv_copy(k + 1).wait_recv()
            kv_pair(k + 1).start()

        kv_pair(k).wait_recv()
        attend(s - k, False)
        return carried

    def attend_some(first, stop):
        lax.fori_loop(first, stop, attend_turn, 0)

    cut1, cut2 = 1 + (s + 1) // 3, 1 + (2 * s + 1) // 3
    attend(s, True)
    loads[2].wait()

    def split_mixer(c):
        def turn(k, carried):
            rows = pl.ds(pl.multiple_of(64 * k, 64), 64)
            w_mix[c, rows, :] = refs.raw[rows, c, :C]
            return carried

        lax.fori_loop(0, D // 64, turn, 0)

    split_mixer(1)
    taps_gather.middle()
    st_gather.middle()

    @pl.when(s > 0)
    def _():
        halo_copy.wait_recv()

    @pl.when(s == 0)
    def _():
        refs.halo_rx[...] = jnp.zeros(refs.halo_rx.shape, BF16)

    hf = refs.halo_rx[...].astype(F32)
    inv_h = lax.rsqrt(jnp.mean(hf * hf, axis=1, keepdims=True) + EPSILON)
    normed[:HALO, :] = (hf * inv_h * ngain).astype(BF16)
    ext_f, ext_s, ext_o = refs.ext_f, refs.ext_s, refs.ext_o
    ext_f[...] = nn(normed[...], w_mix[1]).astype(BF16).astype(F32)
    inner_lin = conv_ref(ext_f, taps_mix, masks, T)
    inner = silu(inner_lin)
    taps_gather.finish()
    st_gather.finish()
    for c in range(2):
        ext_s[...] = nt(normed[...], refs.st_all[c]).astype(BF16).astype(F32)
        taps = refs.taps_all[c].T
        refs.wr[c] = silu(conv_ref(ext_s, taps, masks, T))
    write, read = refs.wr[0], refs.wr[1]
    step = softplus(raw)
    causal = iota((T, T), 0) >= iota((T, T), 1)
    tri = causal.astype(F32)
    cum = nn(tri, -step * rate_row, LEFT)
    cum_t = cum.T
    linked = (doc == doc_row) & causal
    E = expander(C)
    rows_e = expand_rows(C)
    inflow = step * real_col
    inflow_e = nn(inflow, E, RIGHT)
    in_x = inner * inflow_e
    cum_last = cum[T - 1 : T]
    last = first_row + T - 1
    doc_last = doc_of(starts, jnp.full((T, 1), last, jnp.int32))
    prior = doc_of(starts, jnp.full((T, 1), first_row - 1, jnp.int32))
    tail = jnp.where(doc == doc_last, jnp.exp(cum_last - cum), 0.0)
    refs.tail_e[...] = nn(tail, E, RIGHT)
    state_part = tn(refs.tail_e[...] * in_x, write, FINE)
    alive = (doc == prior).astype(F32)
    alive_last = (doc_last == prior).astype(F32)[:8]
    thr = alive_last * jnp.exp(jnp.broadcast_to(cum_last, (8, LANES)))
    steps = carry_steps(n)

    carry = Carry(refs.fc, (refs.window, refs.window_thr), n, s, 1, rows_e)
    carry.begin(state_part, thr)

    g_mat = nt(read, write, FINE)
    for p in range(pairs):
        cols = slice(LANES * p, LANES * (p + 1))
        ys = []
        for h in (2 * p, 2 * p + 1):
            link = link_of(linked, cum, cum_t, h)
            ys.append(nn(link * g_mat, in_x[:, cols], FINE))
        refs.ssd[:, cols] = jnp.where(low, ys[0], ys[1])

    split_mixer(0)
    loads[7].start()
    refs.z[...] = nn(main, w_mix[0])
    for slot in range(min(2, steps)):
        carry.advance(slot)

    @pl.when(s > 0)
    def _():
        kv_copy(1).wait_recv()
        kv_pair(1).start()

    attend_some(1, cut1)
    if steps > 2:
        carry.advance(2)
    attend_some(cut1, cut2)
    carry.rest(3)
    s_in = refs.window[...]
    refs.reach_e[...] = nn(alive * jnp.exp(cum), E, RIGHT)
    ssd = refs.ssd[...] + refs.reach_e[...] * nt(read, s_in, FINE)
    refs.ssd[...] = ssd
    z = refs.z[...]
    full_mix = ssd + skip_row * inner
    gated = full_mix * silu(z)
    copies, wait = share_rows(refs.sq, ns, t, row_sums(gated * gated))
    sent += copies
    attend_some(cut2, s + 1)
    out = acc_ref[...] / l_ref[...]
    acc_ref[...] = out
    m_ref[...] = m_ref[...] + jnp.log(l_ref[...])
    joined[:, :QC] = jnp.where(low, roll(out[:T], HEAD_SIZE), out[T:]).astype(BF16)
    loads[3].wait()
    loads[4].wait()
    loads[5].wait()
    loads[6].wait()
    dh = nn(grad[...], down[...])
    inv_g = as_column(lax.rsqrt(wait() / DM + EPSILON))
    joined[:, QC:] = (gated * inv_g * ggain_row).astype(BF16)
    rs1 = RowScatter(refs.rs1, refs.rs1_sem, t)
    rs1.start(nn(joined[...], w_joint[...]))
    own_rows = pl.ds(pl.multiple_of(TO * t, TO), TO)
    x_own = x[own_rows, :].astype(F32)
    rs1.middle()
    loads[7].wait()

    def split_columns(half):
        columns = slice(F // 2 * half, F // 2 * (half + 1))

        def turn(k, carried):
            rows = pl.ds(pl.multiple_of(64 * k, 64), 64)
            for c in range(2):
                w_gu[c, rows, columns] = refs.raw[rows, c, : F // 2]
            return carried

        lax.fori_loop(0, D // 64, turn, 0)

    split_columns(0)
    loads[8].start()
    res = x_own + rs1.finish()
    inv2 = lax.rsqrt(jnp.mean(res * res, axis=1, keepdims=True) + EPSILON)
    mgain = refs.mgain[...]
    ag1 = gather(refs.ag1_all, refs.ag1_sem, t, (res * inv2 * mgain).astype(BF16))
    loads[8].wait()
    split_columns(1)
    ag1.middle()
    jall = Gather(lambda index: refs.jall_all.at[index], refs.jall, t)
    ag1.finish()

    n2 = jnp.concatenate([refs.ag1_all[k] for k in range(ns)], axis=0)
    gate, up = nn(n2, w_gu[0]), nn(n2, w_gu[1])
    sig = sigmoid(gate)
    act = gate * sig
    hidden = (act * up).astype(BF16)
    d_gate = (dh * up * (sig * (1.0 + gate * (1.0 - sig)))).astype(BF16)
    d_up = (dh * act).astype(BF16)
    rs2 = RowScatter(refs.rs2, refs.rs2_sem, t)
    rs2.start(nt(d_gate, w_gu[0]) + nt(d_up, w_gu[1]))
    for copy in rs1.copies + ag1.copies:
        copy.wait_send()
    rs3 = RowScatter(refs.rs1, refs.rs3_sem, t)
    rs3.start(nt(hidden, down[...]))
    rs2.middle()

    def weight_sum(stream, parts, swapped=False):
        total = HalvingSum(stream, n, s, swapped)
        column = 0
        for lhs, rhs in parts:
            width = rhs.shape[1]
            for c in range(0, width, 256):
                piece = rhs[:, c : min(c + 256, width)]
                total.fill(column + c, tn(lhs, piece).astype(BF16))
            column += width
        return total

    sum_gate = weight_sum(refs.gate_g, [(n2, d_gate)], True)
    sum_gate.start()
    rs3.middle()
    sum_down = weight_sum(refs.down_g, [(grad[...], hidden)])
    sum_down.start()
    sum_up = weight_sum(refs.up_g, [(n2, d_up)])
    dn2 = rs2.finish()
    scaled = dn2 * mgain
    d_res = (
        grad[own_rows, :].astype(F32)
        + inv2 * scaled
        - res * inv2 * inv2 * inv2 * jnp.mean(scaled * res, axis=1, keepdims=True)
    )
    ag2 = gather(refs.ag2_all, refs.ag2_sem, t, d_res.astype(BF16))

    def put_small(row, values):
        for k in range(0, values.shape[1], LANES):
            piece = values[:, k : k + LANES]
            refs.small_tx[row : row + 1, : piece.shape[1]] = piece
            row += 1

    refs.small_tx[...] = jnp.zeros(refs.small_tx.shape, F32)
    refs.step_src[...] = jnp.zeros(refs.step_src.shape, F32)
    put_small(8, jnp.sum(dn2 * res * inv2, axis=0, keepdims=True))
    ag2.middle()
    ag3 = gather(refs.ag1_all, refs.ag3_sem, t, (res + rs3.finish()).astype(BF16))
    ag2.finish()
    d_branch = jnp.concatenate([refs.ag2_all[k] for k in range(ns)], axis=0)
    d_joined = nt(d_branch, w_joint[...])
    d_gn = d_joined[:, QC:]
    scaled = d_gn * ggain_row
    copies, wait = share_rows(refs.dot, ns, t, row_sums(scaled * gated))
    sent += copies
    put_small(16, jnp.sum(d_gn * gated * inv_g, axis=0, keepdims=True))
    d_att = d_joined[:, :QC].astype(BF16).astype(F32)
    dout2 = jnp.concatenate(
        [jnp.where(low, 0.0, roll(d_att, HEAD_SIZE)), jnp.where(low, 0.0, d_att)], axis=0
    )
    delta = jnp.sum(dout2 * acc_ref[...], axis=1, keepdims=True)
    l_ref[...] = delta
    refs.dout2[...] = dout2.astype(BF16)
    jall.middle()
    sum_down.step(0)
    sum_gate.step(0)
    jall.finish()
    own_d = pl.ds(pl.multiple_of((D // ns) * t, LANES), D // ns)
    d_cols = jnp.concatenate([refs.ag2_all[k, :, own_d] for k in range(ns)], axis=0)
    sum_joint = joint = HalvingSum(refs.joint_g, n, s)
    rows_j = joint.src.shape[1]
    piece = min(rows_j, LANES)
    for k in range(ns):
        values = tn(refs.jall_all[k], d_cols).astype(BF16)
        for at in range(0, QC + C, piece):
            row = QC * k + at if at < QC else AQ + C * k + at - QC
            offset = row % rows_j
            joint.src[joint.block_of(row // rows_j), offset : offset + piece, :] = values[at : at + piece]
    dot = as_column(wait() / DM)
    d_gated = inv_g * scaled - gated * (inv_g * inv_g * inv_g * dot)
    sig = sigmoid(z)
    dy = d_gated * z * sig
    refs.d_z[...] = (d_gated * full_mix * (sig * (1.0 + z * (1.0 - sig)))).astype(BF16)
    put_small(19, nt(jnp.broadcast_to(jnp.sum(dy * inner, axis=0, keepdims=True), (8, C)), E, RIGHT)[:1])
    reach_dy = refs.reach_e[...] * dy
    carry_b = Carry(refs.bc, (refs.window, refs.window_thr), n, s, -1, rows_e)
    carry_b.begin(tn(reach_dy, read, FINE), thr)
    sum_up.start()
    joint.start()
    sum_z = weight_sum(refs.z_g, [(main, refs.d_z[...])], True)
    ag3.middle()
    d_g = jnp.zeros((T, T), F32)
    for p in range(pairs):
        cols = slice(LANES * p, LANES * (p + 1))
        xp, dyp = in_x[:, cols], dy[:, cols]
        halves = []
        for k in range(2):
            link = link_of(linked, cum, cum_t, 2 * p + k)
            halves.append(tn(link * g_mat, dyp, FINE))
            own = low if k == 0 else jnp.logical_not(low)
            d_g = d_g + link * nt(jnp.where(own, dyp, 0.0), xp, FINE)
        refs.w_tot[:, cols] = jnp.where(low, halves[0], halves[1])

    d_read = nn(d_g, write, FINE) + nn(reach_dy, s_in, FINE)
    refs.dwr_tx[1] = d_read.T.astype(BF16)
    refs.d_write[...] = tn(d_g, read, FINE)
    refs.dq2[...] = jnp.zeros(refs.dq2.shape, F32)

    def attend_back(j, diagonal):
        block = kv_all[j]
        q2, dout2 = refs.q2[...], refs.dout2[...]
        scores = jnp.where(allowed_at(j, diagonal), nt(q2, block), FAR)
        p = jnp.exp(scores - m_ref[...])
        ds = (p * (nt(dout2, block) - l_ref[...])).astype(BF16)
        refs.dq2[...] += nn(ds, block)
        return tn(ds, q2) + tn(p.astype(BF16), dout2)

    def dkv_copy(k):
        return pltpu.make_async_remote_copy(
            src_ref=refs.dkv_mid.at[k - 1],
            dst_ref=refs.dkv_rx.at[k - 1],
            send_sem=refs.dkv[0].at[k - 1],
            recv_sem=refs.dkv[1].at[k - 1],
            device_id={SEQ: lax.rem(s - k + n, n)},
            device_id_type=MESH,
        )

    def dkv_pair(k):
        return pltpu.make_async_remote_copy(
            src_ref=kv_all.at[s - k, other_half],
            dst_ref=refs.dkv_mid.at[lax.rem(k + n - 1, n)],
            send_sem=refs.dkv_fwd[0].at[k],
            recv_sem=refs.dkv_fwd[1].at[k],
            device_id={STATE: sibling(t)},
            device_id_type=MESH,
        )

    def dkv_on(k):
        dkv_pair(k).wait_recv()
        both = refs.dkv_mid[k - 1].astype(F32) + kv_all[s - k, own_half].astype(F32)
        refs.dkv_mid[k - 1] = both.astype(BF16)
        dkv_copy(k).start()

    def back_turn(k, carried):
        kv_all[s - k] = attend_back(s - k, False).astype(BF16)
        dkv_pair(k).start()

        @pl.when(k > 1)
        def _():
            dkv_on(k - 1)

        return carried

    def back_some(first, stop):
        lax.fori_loop(first, stop, back_turn, 0)

    def kv_end(k, carried):
        kv_copy(k).wait_send()
        return carried

    def pair_end(k, carried):
        kv_pair(k).wait_send()
        return carried

    lax.fori_loop(1, n - s, kv_end, 0)
    lax.fori_loop(1, s + 1, pair_end, 0)
    for slot in range(min(2, steps)):
        carry_b.advance(slot)
    back_some(1, cut1)
    if steps > 2:
        carry_b.advance(2)
    back_some(cut1, cut2)
    carry_b.rest(3)
    back_some(cut2, s + 1)
    diagonal = attend_back(s, True)
    refs.dkv_sum[...] = diagonal
    kv_all[s] = diagonal.astype(BF16)
    dkv_pair(0).start()

    @pl.when(s > 0)
    def _():
        dkv_on(s)

    sum_z.start()
    ag3.finish()
    for k in range(ns):
        refs.layer_output[TO * k : TO * (k + 1), :] = refs.ag1_all[k]
    sum_down.step(1)
    sum_gate.step(1)
    sum_up.step(0)
    later = refs.window[...]
    tail_e = refs.tail_e[...]
    tail_r = tail_e * nt(write, later, FINE)
    w_tot = refs.w_tot[...] + tail_r
    d_write = refs.d_write[...] + nn(tail_e * in_x, later, FINE)
    refs.dwr_tx[0] = d_write.T.astype(BF16)
    dwr = []
    for k in range(1, ns):
        p = lax.rem(t + k, ns)
        theirs = pl.ds(pl.multiple_of(NW * p, NW), NW)
        dwr.append(
            send_to(refs.dwr, k - 1, refs.dwr_tx.at[:, theirs, :], refs.dwr_rx.at[k - 1], {STATE: p})
        )
    sent += dwr
    d_lin = (inflow_e * w_tot + skip_row * dy) * silu_slope(inner_lin)

    def conv_back(ext, grad, taps, up, row, rows):
        grad[...] = jnp.zeros(grad.shape, F32)
        for k in range(KC):
            at = HALO - KC + 1 + k
            masked = up * masks[k]
            put_small(row + rows * k, jnp.sum(masked * ext[at : at + T, :], axis=0, keepdims=True))
            grad[at : at + T, :] += masked * taps[k : k + 1]
        return grad[...].astype(BF16)

    d_ext = conv_back(ext_f, refs.grad_f, taps_mix, d_lin, 22, C // LANES)
    st64 = refs.st_own[...].reshape(2 * NW, D)
    taps_own = refs.taps_st[...].reshape(2 * NW, LANES).T
    ext_o[...] = nt(normed[...], st64).astype(BF16).astype(F32)
    slope_o = silu_slope(conv_ref(ext_o, taps_own, masks, T))
    for copy in dwr:
        copy.wait_recv()
    d_wr = refs.dwr_tx[:, mine, :].astype(F32)
    for k in range(1, ns):
        d_wr = d_wr + refs.dwr_rx[k - 1].astype(F32)
    row_st = 22 + KC * (C // LANES)
    d_st = conv_back(ext_o, refs.grad_o, taps_own, d_wr.reshape(2 * NW, T).T * slope_o, row_st, 1)
    refs.back_tx[...] = (nt(d_ext[:HALO], w_mix[1]) + nn(d_st[:HALO], st64)).astype(BF16)
    def back_copy(member):
        return pltpu.make_async_remote_copy(
            src_ref=refs.back_tx,
            dst_ref=refs.back_rx.at[member],
            send_sem=refs.back[0].at[0],
            recv_sem=refs.back[1].at[member],
            device_id={SEQ: lax.rem(s + n - 1, n), STATE: ns - 1},
            device_id_type=MESH,
        )

    @pl.when(s > 0)
    def _():
        back_copy(t).start()

    sum_inner = weight_sum(refs.inner_g, [(normed[...], d_ext)])
    sum_inner.start()
    u = nt(inner * w_tot, E, RIGHT)
    tl = nt(in_x * tail_r, E, RIGHT)
    thr_s = jnp.sum(tn(later * s_in, rows_e, RIGHT), axis=0, keepdims=True) * thr[:1]
    d_cum = nt(dy * ssd, E, RIGHT) - inflow * u
    at_last = iota((T, LANES), 0) == T - 1
    d_cum = d_cum + jnp.where(at_last, jnp.sum(tl, axis=0, keepdims=True) + thr_s, 0.0)
    d_ld = tn(tri, d_cum, LEFT)
    d_step = real_col * u - rate_row * d_ld
    put_small(20, -jnp.sum(step * d_ld, axis=0, keepdims=True))
    d_step = d_step * sigmoid(raw)
    put_small(21, jnp.sum(d_step, axis=0, keepdims=True))
    d_step = d_step.astype(BF16)
    d_z = refs.d_z[...]
    dq2 = refs.dq2[...]
    dq = jnp.where(low, dq2[:T], roll(dq2[T:], HEAD_SIZE)) * scale
    d_q = rope(dq, cosine, sine, -1.0).astype(BF16)
    d_n = (
        nt(d_z, w_mix[0])
        + nt(d_ext[HALO:], w_mix[1])
        + nn(d_st[HALO:], st64)
        + nn(nt(d_step, pick.astype(BF16)).astype(BF16), w_step[...])
    )
    def dkv_turn(k, carried):
        dkv_copy(k).wait_recv()
        refs.dkv_half[...] += refs.dkv_rx[k - 1].astype(F32)
        return carried

    dkv_pair(0).wait_recv()
    refs.dkv_half[...] = refs.dkv_sum[own_half, :] + refs.dkv_mid[n - 1].astype(F32)
    lax.fori_loop(1, n - s, dkv_turn, 0)
    refs.pair_tx[...] = refs.dkv_half[...].astype(BF16)
    odd = core
    pair = send_to(refs.pair, 0, refs.pair_tx, refs.pair_rx, {STATE: sibling(t)})
    sent.append(pair)
    pair.wait_recv()
    refs.dkv_sum[own_half, :] = refs.pair_tx[...].astype(F32)
    refs.dkv_sum[other_half, :] = refs.pair_rx[...].astype(F32)
    d_kv = rope(refs.dkv_sum[...], kcos, ksin, -1.0)
    d_kv = jnp.where(low == (odd == 0), d_kv, 0.0)
    other = roll(d_kv, HEAD_SIZE)
    d_k = jnp.where(low, jnp.where(group == 0, d_kv, 0.0), jnp.where(group == 0, 0.0, other))
    d_v = jnp.where(low, jnp.where(group == 0, other, 0.0), jnp.where(group == 0, 0.0, d_kv))
    d_kv_b = d_kv.astype(BF16)
    d_qkv = jnp.concatenate([d_q, jnp.where(odd == 0, d_k, d_v).astype(BF16)], axis=1)
    mine_kv = jnp.where(odd == 0, d_kv, other).astype(BF16)
    pad_st = jnp.concatenate([jnp.zeros((T + HALO, HEAD_SIZE), F32), d_st.astype(F32)], axis=1)
    mine_kv = jnp.concatenate([jnp.zeros((HALO, LANES), F32), mine_kv.astype(F32)], axis=0)
    mixed = jnp.where(iota((T + HALO, LANES), 1) < HEAD_SIZE, mine_kv, pad_st).astype(BF16)
    sum_rest = weight_sum(refs.rest_g, [(main, d_q), (normed[...], mixed)])
    sum_rest.start()
    w_kv = jnp.where(odd == 0, w_qkv[:, QC : 2 * QC], w_qkv[:, 2 * QC :])
    d_n = d_n + nt(d_qkv, jnp.concatenate([w_qkv[:, :QC], w_kv], axis=1))
    for copy in rs2.copies + ag3.copies:
        copy.wait_send()
    rs4 = RowScatter(refs.rs2, refs.rs4_sem, t)
    rs4.start(d_n)
    sum_joint.step(0)
    rs4.middle()
    sum_z.step(0)
    sum_up.step(1)
    inv_own = inv1[own_rows, :]
    d_n = rs4.finish()
    last_rows = (t == ns - 1) & (s + 1 < n)

    @pl.when(last_rows)
    def _():
        for member in range(ns):
            back_copy(member).wait_recv()

    @pl.when(jnp.logical_not(last_rows))
    def _():
        refs.back_rx[...] = jnp.zeros(refs.back_rx.shape, BF16)

    from_next = refs.back_rx[0].astype(F32)
    for member in range(1, ns):
        from_next = from_next + refs.back_rx[member].astype(F32)
    d_n = jnp.concatenate([d_n[: TO - HALO], d_n[TO - HALO :] + from_next], axis=0)
    scaled = d_n * ngain
    in_g = (
        d_res
        + inv_own * scaled
        - x_own * inv_own * inv_own * inv_own * jnp.mean(scaled * x_own, axis=1, keepdims=True)
    )
    ag4 = gather(refs.ag1_all, refs.ag4_sem, t, in_g.astype(BF16))
    put_small(0, jnp.sum(d_n * x_own * inv_own, axis=0, keepdims=True))

    def small_copy(k):
        peer = lax.rem(s + k, n)
        make = lambda src, dst, at: pltpu.make_async_remote_copy(
            src_ref=src,
            dst_ref=dst,
            send_sem=refs.small[0].at[at],
            recv_sem=refs.small[1].at[at],
            device_id={SEQ: peer},
            device_id_type=MESH,
        )
        return (
            make(refs.small_tx, refs.small_rx.at[s, pl.ds(0, rows_c)], k - 1),
            make(refs.step_src.at[peer], refs.small_rx.at[s, pl.ds(rows_c, 8)], n + k - 2),
        )

    step_rows = tn(d_step, main)[:8]
    rows_c, rows_d = refs.small_tx.shape[0], D // n
    for k in range(n):
        refs.step_src[k, :, :rows_d] = step_rows[:, rows_d * k : rows_d * (k + 1)]
    refs.small_rx[s, :rows_c, :] = refs.small_tx[...]
    refs.small_rx[s, rows_c:, :] = refs.step_src[s]

    def small_turn(k, carried):
        for copy in small_copy(k):
            copy.start()
        return carried

    lax.fori_loop(1, n, small_turn, 0)
    last_level = len(bits_of(n, False)) - 1

    def steps_of(total, first, stop):
        for level in range(first, stop):
            total.step(level)

    sum_inner.step(0)
    sum_z.step(1)
    ag4.middle()
    sum_joint.step(1)
    sum_rest.step(0)
    steps_of(sum_down, 2, last_level + 1)
    steps_of(sum_gate, 2, last_level + 1)
    ag4.finish()
    for k in range(ns):
        refs.input_grad[TO * k : TO * (k + 1), :] = refs.ag1_all[k]
    steps_of(sum_up, 2, last_level + 1)
    steps_of(sum_z, 2, last_level + 1)
    gz = gather(refs.gz_all, refs.gz_sem, t, sum_z.result())
    sum_inner.step(1)
    steps_of(sum_joint, 2, last_level + 1)
    gj = gather(refs.gj_all, refs.gj_sem, t, sum_joint.result())
    sum_rest.step(1)
    gz.middle()
    steps_of(sum_inner, 2, last_level + 1)
    gi = gather(refs.gi_all, refs.gi_sem, t, sum_inner.result())
    gj.middle()
    steps_of(sum_rest, 2, last_level + 1)
    gr = gather(refs.gr_all, refs.gr_sem, t, sum_rest.result())

    def small_end(k, carried):
        for copy in small_copy(k):
            copy.wait_recv()
        return carried

    lax.fori_loop(1, n, small_end, 0)

    def small_sum(j, total):
        return total + refs.small_rx[j]

    small = gather(
        refs.sm_all, refs.sm_sem, t,
        lax.fori_loop(0, n, small_sum, jnp.zeros(refs.small_rx.shape[1:], F32)),
    )
    gi.middle()
    small.middle()
    refs.o_gu[0] = sum_gate.result()
    refs.o_gu[1] = sum_up.result()
    refs.o_down[...] = sum_down.result()
    gz.finish()
    gj.finish()
    gi.finish()
    gr.middle()
    for k in range(ns):
        refs.o_mix[0, :, C * k : C * (k + 1)] = refs.gz_all[k]
        refs.o_mix[1, :, C * k : C * (k + 1)] = refs.gi_all[k]
        refs.o_joint[:, (D // ns) * k : (D // ns) * (k + 1)] = refs.gj_all[k]
    small.finish()
    total = refs.sm_all[0, :16, :]
    for k in range(1, ns):
        total = total + refs.sm_all[k, :16, :]
    refs.o_gains[...] = total
    refs.o_small[...] = refs.sm_all[:, 16:rows_c, :]
    gr.finish()
    rows = refs.gr_all.shape[1]
    half = iota((rows, LANES), 1) < HEAD_SIZE
    for k in range(ns):
        refs.o_att[:, QC * k : QC * (k + 1)] = refs.gr_all[k, :, :QC]
        refs.o_step[HL * k : HL * (k + 1), :] = refs.sm_all[k, rows_c : rows_c + HL, :rows]
    for c in range(2):
        first = refs.gr_all[c, :, QC : 2 * QC].astype(F32)
        second = refs.gr_all[2 + c, :, QC : 2 * QC].astype(F32)
        refs.o_att[:, AQ + QC * c : AQ + QC * (c + 1)] = jnp.where(
            half, first, roll(second, HEAD_SIZE)
        ).astype(BF16)
    refs.o_st[...] = refs.gr_all[t, :, QC : 2 * QC]

    def small_sent(k, carried):
        for copy in small_copy(k):
            copy.wait_send()
        return carried

    lax.fori_loop(1, n, small_sent, 0)
    for group_of in (
        st_gather, taps_gather, jall, rs3, rs4, ag2, ag4, gz, gj, gi, gr, small,
        sum_gate, sum_up, sum_down, sum_z, sum_joint, sum_inner, sum_rest,
    ):
        sent += group_of.copies
    for copy in sent:
        copy.wait_send()

    @pl.when(s + 1 < n)
    def _():
        halo_copy.wait_send()

    @pl.when(s > 0)
    def _():
        back_copy(t).wait_send()

    carry.finish()
    carry_b.finish()

    def dkv_end(k, carried):
        dkv_copy(k).wait_send()
        return carried

    def dkv_pair_end(k, carried):
        dkv_pair(k).wait_send()
        return carried

    lax.fori_loop(1, s + 1, dkv_end, 0)
    lax.fori_loop(0, s + 1, dkv_pair_end, 0)


def layer(n, ns, arrays):
    inputs = types.SimpleNamespace(**arrays)
    T, D = inputs.x.shape
    C = inputs.w_mix_in.shape[2] // ns
    NW = inputs.st_own.shape[1]
    F = inputs.down_in.shape[1]
    N, TO, H = NW * ns, T // ns, NH // ns
    KJ = inputs.joint.shape[0]
    QC = 2 * HEAD_SIZE
    R, RJ = D // n, KJ // n
    steps = carry_steps(n)
    levels = levels_of(n)
    sd = jax.ShapeDtypeStruct
    J = QC + C
    SMALL = -(-(22 + KC * (C // LANES) + KC) // 8) * 8
    outs = dict(
        layer_output=sd((T, D), BF16),
        input_grad=sd((T, D), BF16),
        o_down=sd((R, F), BF16),
        o_gu=sd((2, R, F), BF16),
        o_mix=sd((2, R, ns * C), BF16),
        o_joint=sd((RJ, D), BF16),
        o_att=sd((R, inputs.w_att.shape[1]), BF16),
        o_step=sd((NH, R), F32),
        o_st=sd((R, LANES), BF16),
        o_gains=sd((16, LANES), F32),
        o_small=sd((ns, SMALL - 16, LANES), F32),
    )
    vm = pltpu.VMEM
    dma = lambda k: (pltpu.SemaphoreType.DMA((k,)), pltpu.SemaphoreType.DMA((k,)))
    blocks = lambda *shape: vm((ns,) + shape, BF16)

    def scan():
        return dict(
            tx=vm((max(1, steps - 1), C, N), BF16),
            rx=vm((steps, C, N), BF16),
            thr_tx=vm((max(1, steps - 1), 8, LANES), F32),
            thr_rx=vm((steps, 8, LANES), F32),
            sem=dma(steps),
            thr_sem=dma(steps),
        )

    def rows():
        return dict(tx=vm((8, T), F32), rx=vm((ns - 1, 8, T), F32), sem=dma(ns - 1))

    def scatter():
        return dict(tx=blocks(TO, D), rx=vm((3, TO, D), BF16), mid=vm((TO, D), BF16))

    def stream(*shape):
        return dict(src=vm((n,) + shape, BF16), rx=vm((n - 1,) + shape, BF16), sem=dma(levels))

    scratch = dict(
        w_qkv=vm((D, 3 * QC), BF16),
        w_joint=vm((J, D), BF16),
        w_mix=vm((2, D, C), BF16),
        w_gu=vm((2, D, F), BF16),
        raw=vm((D, 2, max(C, F // 2)), BF16),
        down=vm((D, F), BF16),
        grad=vm((T, D), BF16),
        load=tuple(pltpu.SemaphoreType.DMA for _ in range(9)),
        taps8=vm((8, LANES), F32),
        taps_st=vm((2, NW, LANES), F32),
        codes=vm((n * T // LANES, LANES), jnp.int32),
        halo_rx=vm((HALO, D), BF16),
        st_all=vm((2, N, D), BF16),
        taps_all=vm((2, N, LANES), F32),
        kv_all=vm((n, T, LANES), BF16),
        normed=vm((T + HALO, D), BF16),
        inv1=vm((T, 1), F32),
        q2=vm((2 * T, LANES), BF16),
        z=vm((T, C), F32),
        ext_f=vm((T + HALO, C), F32),
        ext_s=vm((T + HALO, N), F32),
        ext_o=vm((T + HALO, 2 * NW), F32),
        grad_f=vm((T + HALO, C), F32),
        grad_o=vm((T + HALO, 2 * NW), F32),
        wr=vm((2, T, N), F32),
        tail_e=vm((T, C), F32),
        reach_e=vm((T, C), F32),
        ssd=vm((T, C), F32),
        w_tot=vm((T, C), F32),
        d_z=vm((T, C), BF16),
        jall_all=vm((ns, T, J), BF16),
        window=vm((C, N), F32),
        window_thr=vm((8, LANES), F32),
        m_acc=vm((2 * T, 1), F32),
        l_acc=vm((2 * T, 1), F32),
        o_acc=vm((2 * T, LANES), F32),
        dout2=vm((2 * T, LANES), BF16),
        dq2=vm((2 * T, LANES), F32),
        dkv_rx=vm((n, T // 2, LANES), BF16),
        dkv_mid=vm((n, T // 2, LANES), BF16),
        dkv_half=vm((T // 2, LANES), F32),
        dkv_sum=vm((T, LANES), F32),
        pair_tx=vm((T // 2, LANES), BF16),
        pair_rx=vm((T // 2, LANES), BF16),
        back_tx=vm((HALO, D), BF16),
        back_rx=vm((ns, HALO, D), BF16),
        dwr_tx=vm((2, N, T), BF16),
        d_write=vm((T, N), F32),
        dwr_rx=vm((ns - 1, 2, NW, T), BF16),
        small_tx=vm((SMALL, LANES), F32),
        step_src=vm((n, 8, LANES), F32),
        small_rx=vm((n, SMALL + 8, LANES), F32),
        halo=dma(1),
        st=dma(3),
        taps=dma(3),
        kv=dma(n - 1),
        kv_fwd=dma(n - 1),
        dkv=dma(n - 1),
        dkv_fwd=dma(n),
        jall=dma(3),
        pair=dma(1),
        back=dma(ns),
        dwr=dma(ns - 1),
        small=dma(2 * n - 2),
        sm_all=vm((ns, SMALL + 8, LANES), F32),
        fc=scan(),
        bc=scan(),
        sq=rows(),
        dot=rows(),
        rs1=scatter(),
        rs2=scatter(),
        rs1_sem=dma(2),
        rs2_sem=dma(2),
        rs3_sem=dma(2),
        rs4_sem=dma(2),
        ag1_all=blocks(TO, D),
        ag2_all=blocks(TO, D),
        gz_all=blocks(R, C),
        gi_all=blocks(R, C),
        gr_all=blocks(R, 2 * LANES),
        gj_all=blocks(RJ, D // ns),
        ag1_sem=dma(3),
        ag2_sem=dma(3),
        ag3_sem=dma(3),
        ag4_sem=dma(3),
        gz_sem=dma(3),
        gi_sem=dma(3),
        gr_sem=dma(3),
        gj_sem=dma(3),
        sm_sem=dma(3),
        gate_g=stream(R, F),
        up_g=stream(R, F),
        down_g=stream(R, F),
        z_g=stream(R, C),
        inner_g=stream(R, C),
        rest_g=stream(R, 2 * LANES),
        joint_g=stream(RJ, D // ns),
    )
    whole = pl.BlockSpec(memory_space=pltpu.VMEM)
    small = pl.BlockSpec(memory_space=pltpu.SMEM)
    far = pl.BlockSpec(memory_space=pl.ANY)
    specs = {key: whole for key in arrays}
    specs.update(doc_starts=small, step_bias=small, decay_rate=small, skip_gain=small)
    specs.update(w_att=far, joint=far, g=far, w_mix_in=far, w_gu_in=far, down_in=far)
    flat = [jax.tree.flatten(group) for group in (arrays, outs, scratch)]
    got = pl.pallas_call(
        functools.partial(layer_kernel, n, ns, [tree for _, tree in flat]),
        out_shape=flat[1][0],
        in_specs=jax.tree.flatten(specs)[0],
        out_specs=[whole] * len(outs),
        scratch_shapes=flat[2][0],
        name="layer",
        compiler_params=pltpu.CompilerParams(
            collective_id=1, has_side_effects=True, vmem_limit_bytes=VMEM_LIMIT
        ),
    )(*flat[0][0])
    return types.SimpleNamespace(**jax.tree.unflatten(flat[1][1], got))


def finish_kernel(n, ns, tree_in, tree_out, *flat):
    split = tree_in.num_leaves
    o = named(jax.tree.unflatten(tree_in, flat[:split]))
    out = named(jax.tree.unflatten(tree_out, flat[split:]))
    t, s = lax.axis_index(STATE), lax.axis_index(SEQ)
    HL, C = NH // ns, NH * HDM // ns
    per = C // LANES
    NW = out.taps_st.shape[2]
    R = out.down.shape[0]
    out.layer_output[...] = o.layer_output[...]
    out.input_grad[...] = o.input_grad[...].astype(F32)
    out.att[...] = o.o_att[...].astype(F32)
    out.joint[...] = o.o_joint[...].astype(F32)
    out.down[...] = o.o_down[...].astype(F32)
    out.step[...] = o.o_step[...]
    turned = o.o_st[...].astype(F32).T
    for c in range(2):
        out.mix[:, c, :] = o.o_mix[c].astype(F32)
        out.gu[:, c, :] = o.o_gu[c].astype(F32)
        at = HEAD_SIZE + NW * c
        out.st[c] = turned[at : at + NW]
    small = o.o_small

    def part(row, width, count):
        at = s * width
        first = at // LANES
        lanes = jnp.concatenate([row(first + k) for k in range(count)], axis=1)
        return roll(lanes, lax.rem(count * LANES - (at - first * LANES), count * LANES))[:, :width]

    for at, dst in ((0, out.ngain), (8, out.mgain)):
        dst[...] = part(lambda k: o.o_gains[pl.ds(at + k, 1), :], R, 1)
    for k in range(ns):
        for i in range(per):
            out.gains[per * k + i : per * k + i + 1, :] = small[k, i : i + 1, :]
    width = out.ggain.shape[1]
    last = ns * per - 1
    out.ggain[...] = part(lambda k: out.gains[pl.ds(jnp.minimum(k, last), 1), :], width, 3)
    heads = 0.0
    for k in range(ns):
        into = (iota((LANES, LANES), 1) == HL * k + iota((LANES, LANES), 0)) & (
            iota((LANES, LANES), 0) < HL
        )
        heads = heads + nn(small[k, :8, :], into.astype(F32), RIGHT)
        for j in range(KC):
            for i in range(per):
                row = 6 + per * j + i
                at = C * k + LANES * i
                out.taps[j : j + 1, at : at + LANES] = small[k, row : row + 1, :]
    out.skip[...], out.rate[...], out.bias[...] = (heads[k : k + 1, :NH] for k in (3, 4, 5))
    for j in range(KC):
        row = small[t, 6 + KC * per + j : 7 + KC * per + j, :]
        for c in range(2):
            out.taps_st[j, c : c + 1, :] = row[:, NW * c : NW * (c + 1)]


def finish(n, ns, o, shapes):
    sd = lambda *shape: jax.ShapeDtypeStruct(shape, F32)
    R, F = o.o_down.shape
    T, D = o.layer_output.shape
    NW = shapes.NW
    outs = dict(
        layer_output=jax.ShapeDtypeStruct((T, D), BF16),
        input_grad=sd(T, D),
        att=sd(*o.o_att.shape),
        joint=sd(*o.o_joint.shape),
        down=sd(R, F),
        step=sd(NH, R),
        mix=sd(R, 2, NH * HDM),
        gu=sd(R, 2, F),
        st=sd(2, NW, R),
        ngain=sd(1, R),
        mgain=sd(1, R),
        ggain=sd(1, NH * HDM // n),
        gains=sd(NH * HDM // LANES, LANES),
        taps=sd(KC, NH * HDM),
        taps_st=sd(KC, 2, NW),
        skip=sd(1, NH),
        rate=sd(1, NH),
        bias=sd(1, NH),
    )
    arrays = dict(o.__dict__)
    flat = [jax.tree.flatten(group) for group in (arrays, outs)]
    whole = pl.BlockSpec(memory_space=pltpu.VMEM)
    got = pl.pallas_call(
        functools.partial(finish_kernel, n, ns, flat[0][1], flat[1][1]),
        out_shape=flat[1][0],
        in_specs=[whole] * len(arrays),
        out_specs=[whole] * len(outs),
        name="finish",
        compiler_params=pltpu.CompilerParams(vmem_limit_bytes=VMEM_LIMIT),
    )(*flat[0][0])
    return types.SimpleNamespace(**jax.tree.unflatten(flat[1][1], got))


def local(
    layer_input,
    out_grad,
    doc_starts,
    real_mask,
    norm_gain,
    attention_input_rows,
    mixer_in,
    state_in,
    step_in,
    conv_mixer,
    conv_state,
    step_bias,
    decay_rate,
    skip_gain,
    gated_gain,
    joint_out,
    mlp_gain,
    gate_up,
    down_weight,
):
    T, D = layer_input.shape
    NS, n = lax.axis_size(STATE), lax.axis_size(SEQ)
    NW = state_in.shape[2]
    o = layer(
        n,
        NS,
        dict(
            x=layer_input,
            g=out_grad,
            w_att=attention_input_rows,
            w_mix_in=mixer_in,
            w_step=step_in.T,
            st_own=jnp.transpose(state_in, (1, 2, 0)),
            conv_state=conv_state,
            conv_mixer=conv_mixer,
            ngain=norm_gain[None, :],
            ggain=gated_gain.reshape(-1, LANES),
            mgain=mlp_gain[None, :],
            joint=joint_out,
            w_gu_in=gate_up,
            down_in=down_weight,
            real=real_mask.reshape(-1, LANES),
            step_bias=step_bias,
            decay_rate=decay_rate,
            skip_gain=skip_gain,
            doc_starts=doc_starts,
        ),
    )
    e = finish(n, NS, o, types.SimpleNamespace(NW=NW))
    return (
        e.layer_output,
        e.input_grad,
        e.ngain.reshape(-1),
        e.att,
        e.mix,
        e.st.transpose(2, 0, 1),
        e.step.T,
        e.taps,
        e.taps_st,
        e.bias.reshape(-1),
        e.rate.reshape(-1),
        e.skip.reshape(-1),
        e.ggain.reshape(-1),
        e.joint,
        e.mgain.reshape(-1),
        e.gu,
        e.down,
    )


def solution(mesh):
    rep = P()
    in_specs = (
        P(SEQ, None),
        P(SEQ, None),
        rep,
        rep,
        rep,
        rep,
        rep,
        P(None, None, STATE),
        rep,
        rep,
        P(None, None, STATE),
        rep,
        rep,
        rep,
        rep,
        rep,
        rep,
        P(None, None, STATE),
        P(None, STATE),
    )
    out_specs = (
        P(SEQ, None),
        P(SEQ, None),
        P(SEQ),
        P(SEQ, None),
        P(SEQ, None, None),
        P(SEQ, None, STATE),
        P(SEQ, None),
        rep,
        P(None, None, STATE),
        rep,
        rep,
        rep,
        P(SEQ),
        P(SEQ, None),
        P(SEQ),
        P(SEQ, None, STATE),
        P(SEQ, STATE),
    )
    return jax.shard_map(local, mesh=mesh, in_specs=in_specs, out_specs=out_specs, check_vma=False)
```

profile of v0, /device:TPU:0, one launch (start us, length us, event | category | flops | bytes accessed | tf_op | source)
XLA Modules:
  0.0 153.8 jit_solution(16657674959666032732)
XLA Ops:
  0.7 148.5 %layer.1 = (bf16[256,1024]{1,0:T(8,128)(2,1)}, bf16[256,1024]{1,0:T(8,128)(2,1)}, bf16[128,768]{1,0:T(8,128)(2,1)}, bf16[128,512]{1,0:T(8,128)(2,1)}, f32[16,128...) custom-call(f32[4,1536]{1,0:T(4,128)} %flat_0_.1, ...), custom_call_target="tpu_custom_call" | custom-call | tf_op jit(solution)/shard_map/layer/pallas_call | solution.py:1419
  149.2 4.5 %finish.1 = (f32[128,768]{1,0:T(8,128)}, f32[1,24]{1,0:T(1,128)}, f32[128,512]{1,0:T(8,128)}, f32[12,128]{1,0:T(8,128)}, f32[1,192]{1,0:T(1,128)}, /*index=5*/f3...) custom-call(bf16[256,1024]{1,0:T(8,128)(2,1)} %get-tuple-element.45., ...), custom_call_target="tpu_custom_call" | custom-call | tf_op jit(solution)/shard_map/finish/pallas_call | solution.py:1516
where the time goes:
time: 154 us
  Pallas kernels  153 us (99%)
    pallas_call x1, Pallas kernels, layer(): pl.pallas_call(functools.partial(layer_kernel, n, ns, [tree for _, tree i...  149 us
    pallas_call x1, Pallas kernels, finish(): pl.pallas_call(functools.partial(finish_kernel, n, ns, flat[0][1], flat[1...  4.49 us

commit v1 on v0

--- a/solution.py
+++ b/solution.py
@@ -890,9 +890,9 @@
             d_g = d_g + link * nt(jnp.where(own, dyp, 0.0), xp, FINE)
         refs.w_tot[:, cols] = jnp.where(low, halves[0], halves[1])
 
-    d_read = nn(d_g, write, FINE) + nn(reach_dy, s_in, FINE)
+    d_read = nn(d_g, write) + nn(reach_dy, s_in)
     refs.dwr_tx[1] = d_read.T.astype(BF16)
-    refs.d_write[...] = tn(d_g, read, FINE)
+    refs.d_write[...] = tn(d_g, read)
     refs.dq2[...] = jnp.zeros(refs.dq2.shape, F32)
 
     def attend_back(j, diagonal):
@@ -981,7 +981,7 @@
     tail_e = refs.tail_e[...]
     tail_r = tail_e * nt(write, later, FINE)
     w_tot = refs.w_tot[...] + tail_r
-    d_write = refs.d_write[...] + nn(tail_e * in_x, later, FINE)
+    d_write = refs.d_write[...] + nn(tail_e * in_x, later)
     refs.dwr_tx[0] = d_write.T.astype(BF16)
     dwr = []
     for k in range(1, ns):
@@ -1430,25 +1430,41 @@
     return types.SimpleNamespace(**jax.tree.unflatten(flat[1][1], got))
 
 
-def finish_kernel(n, ns, tree_in, tree_out, *flat):
+def finish_kernel(n, ns, tree_in, tree_out, tree_big, *flat):
     split = tree_in.num_leaves
     o = named(jax.tree.unflatten(tree_in, flat[:split]))
-    out = named(jax.tree.unflatten(tree_out, flat[split:]))
+    last = split + tree_out.num_leaves
+    out = named(jax.tree.unflatten(tree_out, flat[split:last]))
+    held = named(jax.tree.unflatten(tree_big, flat[last:-1]))
+    copies = []
+
+    def leave(src, dst):
+        copies.append(pltpu.make_async_copy(src, dst, flat[-1].at[len(copies)]))
+        copies[-1].start()
+
     t, s = lax.axis_index(STATE), lax.axis_index(SEQ)
     HL, C = NH // ns, NH * HDM // ns
     per = C // LANES
     NW = out.taps_st.shape[2]
     R = out.down.shape[0]
+    for c in range(2):
+        held.mix[:, c, :] = o.o_mix[c].astype(F32)
+    leave(held.mix, out.mix)
+    held.input_grad[...] = o.input_grad[...].astype(F32)
+    leave(held.input_grad, out.input_grad)
+    held.joint[...] = o.o_joint[...].astype(F32)
+    leave(held.joint, out.joint)
+    for c in range(2):
+        held.gu[:, c, :] = o.o_gu[c].astype(F32)
+    leave(held.gu, out.gu)
+    held.att[...] = o.o_att[...].astype(F32)
+    leave(held.att, out.att)
+    held.down[...] = o.o_down[...].astype(F32)
+    leave(held.down, out.down)
     out.layer_output[...] = o.layer_output[...]
-    out.input_grad[...] = o.input_grad[...].astype(F32)
-    out.att[...] = o.o_att[...].astype(F32)
-    out.joint[...] = o.o_joint[...].astype(F32)
-    out.down[...] = o.o_down[...].astype(F32)
     out.step[...] = o.o_step[...]
     turned = o.o_st[...].astype(F32).T
     for c in range(2):
-        out.mix[:, c, :] = o.o_mix[c].astype(F32)
-        out.gu[:, c, :] = o.o_gu[c].astype(F32)
         at = HEAD_SIZE + NW * c
         out.st[c] = turned[at : at + NW]
     small = o.o_small
@@ -1483,6 +1499,8 @@
         row = small[t, 6 + KC * per + j : 7 + KC * per + j, :]
         for c in range(2):
             out.taps_st[j, c : c + 1, :] = row[:, NW * c : NW * (c + 1)]
+    for copy in copies:
+        copy.wait()
 
 
 def finish(n, ns, o, shapes):
@@ -1511,13 +1529,21 @@
         bias=sd(1, NH),
     )
     arrays = dict(o.__dict__)
-    flat = [jax.tree.flatten(group) for group in (arrays, outs)]
+    big = dict(
+        input_grad=outs["input_grad"], att=outs["att"], joint=outs["joint"], down=outs["down"],
+        mix=outs["mix"], gu=outs["gu"],
+    )
+    held = {key: pltpu.VMEM(value.shape, F32) for key, value in big.items()}
+    flat = [jax.tree.flatten(group) for group in (arrays, outs, held)]
     whole = pl.BlockSpec(memory_space=pltpu.VMEM)
+    far = pl.BlockSpec(memory_space=pl.ANY)
+    specs = {key: far if key in big else whole for key in outs}
     got = pl.pallas_call(
-        functools.partial(finish_kernel, n, ns, flat[0][1], flat[1][1]),
+        functools.partial(finish_kernel, n, ns, flat[0][1], flat[1][1], flat[2][1]),
         out_shape=flat[1][0],
         in_specs=[whole] * len(arrays),
-        out_specs=[whole] * len(outs),
+        out_specs=jax.tree.flatten(specs)[0],
+        scratch_shapes=flat[2][0] + [pltpu.SemaphoreType.DMA((len(big),))],
         name="finish",
         compiler_params=pltpu.CompilerParams(vmem_limit_bytes=VMEM_LIMIT),
     )(*flat[0][0])

time: 154 us -> 155 us (level)
  no operation moved by 1% of the time
where the time goes in v1:
time: 155 us
  Pallas kernels  154 us (99%)
    pallas_call x1, Pallas kernels, layer(): pl.pallas_call(functools.partial(layer_kernel, n, ns, [tree for _, tree i...  149 us
    pallas_call x1, Pallas kernels, finish(): pl.pallas_call(functools.partial(finish_kernel, n, ns, flat[0][1], flat[1...  5.46 us

profile of v1, /device:TPU:0, one launch (start us, length us, event | category | flops | bytes accessed | tf_op | source)
XLA Modules:
  0.0 154.9 jit_solution(17934695008785432580)
XLA Ops:
  0.7 148.6 %layer.1 = (bf16[256,1024]{1,0:T(8,128)(2,1)}, bf16[256,1024]{1,0:T(8,128)(2,1)}, bf16[128,768]{1,0:T(8,128)(2,1)}, bf16[128,512]{1,0:T(8,128)(2,1)}, f32[16,128...) custom-call(f32[4,1536]{1,0:T(4,128)} %flat_0_.1, ...), custom_call_target="tpu_custom_call" | custom-call | tf_op jit(solution)/shard_map/layer/pallas_call | solution.py:1419
  149.2 5.5 %finish.1 = (f32[128,768]{1,0:T(8,128)}, f32[1,24]{1,0:T(1,128)}, f32[128,512]{1,0:T(8,128)}, f32[12,128]{1,0:T(8,128)}, f32[1,192]{1,0:T(1,128)}, /*index=5*/f3...) custom-call(bf16[256,1024]{1,0:T(8,128)(2,1)} %get-tuple-element.45., ...), custom_call_target="tpu_custom_call" | custom-call | tf_op jit(solution)/shard_map/finish/pallas_call | solution.py:1541
